TPU v7x, 256 devices: a whole 4x4x8 slice. The times are simulated.
256 devices in a mesh: ctx: 16 (over y_hi, x, core), exp: 8 (over z), dp: 2 (over y_lo).
Axes of the slice: x: 4, y: 4 (y_hi: 2, y_lo: 2; y = y_hi * 2 + y_lo), z: 8, core: 2. Of those that a mesh axis runs over, the one named last changes fastest.
Arguments:
- tokens: bfloat16 [2, 2048, 4096], P('dp', 'ctx'), may hold values from -6 to 6
- norm_in: bfloat16 [4096], replicated, may hold values from 0.099609375 to 1.8984375
- w_qkv: bfloat16 [4096, 8, 6, 128], P('dp', 'exp')
- w_out: bfloat16 [8, 4, 128, 4096], P('exp', None, None, 'dp'), may hold values from -0.375 to 0.375
- norm_mid: bfloat16 [4096], replicated, may hold values from 0.099609375 to 1.8984375
- w_router: bfloat16 [4096, 8], replicated, may hold values from -0.09375 to 0.09375
- w_gate_up: bfloat16 [8, 4096, 2, 8192], P('exp', 'dp', None, 'ctx'), may hold values from -0.09375 to 0.09375
- w_down: bfloat16 [8, 8192, 4096], P('exp', 'ctx', 'dp'), may hold values from -0.0625 to 0.0625
- expert_ids: int32 [2, 2048, 2], P('dp', ('ctx', 'exp')), may hold values from 0 to 7, as said below
- slot_index: int32 [2, 2048, 2], P('dp', ('ctx', 'exp')), may hold values from 0 to 5, as said below
Outputs:
- layer_out: bfloat16 [2, 2048, 4096], P('dp', ('ctx', 'exp'))
Inputs may be any that keep to these rules, and one draw needn't show every extreme that they name: `expert_ids`: each token names two different experts; in every aligned block of 16 tokens (the tokens of one device) the numbers of choices of the experts are, in some order, 6, 5, 4, 4, 4, 3, 3 and 3, so that no expert is named more than 6 times and one exactly 6 times. `slot_index`: a choice's slot is the number of earlier choices of the same expert in its block of 16 tokens, a token's first choice counting before its second.
All inputs are finite; a program needn't handle non-finite values.
Results may differ from a plain program's by a relative error of at most 0.022.
The roundings to bfloat16 on the way count: a program that leaves them out, or rounds other values in their place, can miss the bound.
Values may be sent and summed in bfloat16 or wider, within the bound.
No kernel may reach another device: no remote copies, remote signals or barrier semaphores. Data moves between devices by JAX's collectives and lax.ppermute only.
A program may use at most 128 MiB of HBM per device.

v0:
```python
import math

import jax
import jax.numpy as jnp
from jax import lax
from jax.sharding import PartitionSpec as P

EPSILON = 1e-05
ROPE_BASE = 1000000.0


def rms_norm(values, gain):
    wide = values.astype(jnp.float32)
    square_mean = jnp.mean(wide * wide, axis=-1, keepdims=True)
    return (wide * lax.rsqrt(square_mean + EPSILON) * gain.astype(jnp.float32)).astype(jnp.bfloat16)


def rope_angles(positions, head_dim):
    half_dim = head_dim // 2
    freqs = jnp.exp(
        jnp.arange(half_dim, dtype=jnp.float32) * (-2.0 * math.log(ROPE_BASE) / head_dim)
    )
    return positions[:, None] * freqs[None, :]


def rotate(tensor, angles):
    half_dim = tensor.shape[-1] // 2
    first_half = tensor[..., :half_dim]
    second_half = tensor[..., half_dim:]
    cosine = jnp.cos(angles)
    sine = jnp.sin(angles)
    return jnp.concatenate(
        [first_half * cosine - second_half * sine, second_half * cosine + first_half * sine],
        axis=-1,
    )


def on_device(
    tokens, norm_in, w_qkv, w_out, norm_mid, w_router, w_gate_up, w_down, expert_ids, slot_index
):
    tok_rows = tokens.shape[1]
    head_dim = w_qkv.shape[3]
    kv_local = w_qkv.shape[1]
    group_size = w_qkv.shape[2] - 2
    width = tokens.shape[2]
    normed = rms_norm(tokens, norm_in)
    qkv_full, out_full, gate_up_all, down_all = (
        lax.all_gather(w_qkv, "dp", axis=0, tiled=True),
        lax.all_gather(w_out, "dp", axis=3, tiled=True),
        lax.all_gather(w_gate_up, "dp", axis=1, tiled=True),
        lax.all_gather(w_down, "dp", axis=2, tiled=True),
    )
    projected = jnp.dot(normed[0], qkv_full.reshape(width, -1), preferred_element_type=jnp.float32)[
        None
    ]
    projected = projected.reshape(1, tok_rows, kv_local, group_size + 2, head_dim)
    query_idx = lax.axis_index("ctx") * tok_rows + jnp.arange(tok_rows, dtype=jnp.int32)
    angles = rope_angles(query_idx.astype(jnp.float32), head_dim)
    queries = rotate(projected[:, :, :, :group_size, :], angles[None, :, None, None, :]).astype(
        jnp.bfloat16
    )
    keys_rot = rotate(projected[:, :, :, group_size, :], angles[None, :, None, :]).astype(
        jnp.bfloat16
    )
    values = projected[:, :, :, group_size + 1, :].astype(jnp.bfloat16)
    scale = 1.0 / math.sqrt(head_dim)
    last_query = lax.axis_index("ctx") * tok_rows + tok_rows - 1
    peak_init = jnp.full((1, kv_local, group_size, tok_rows), -1e30, jnp.float32)
    total_init = jnp.zeros((1, kv_local, group_size, tok_rows), jnp.float32)
    accum_init = jnp.zeros((1, kv_local, group_size, tok_rows, head_dim), jnp.float32)
    key_piece = lax.all_gather(keys_rot, "ctx", axis=1, tiled=True)
    value_piece = lax.all_gather(values, "ctx", axis=1, tiled=True)
    count = key_piece.shape[1]

    def compute(state):
        peak, totals, accum = state
        score_matrix = (
            jnp.einsum("bqkgd,bskd->bkgqs", queries, key_piece, preferred_element_type=jnp.float32)
            * scale
        )
        key_idx = jnp.arange(count, dtype=jnp.int32)
        causal = key_idx[None, :] <= query_idx[:, None]
        score_matrix = jnp.where(causal, score_matrix, -1e30)
        new_peak = jnp.maximum(peak, jnp.max(score_matrix, axis=-1))
        probs = jnp.where(causal, jnp.exp(score_matrix - new_peak[..., None]), 0.0)
        totals = jnp.sum(probs, axis=-1)
        update = jnp.einsum(
            "bkgqs,bskd->bkgqd",
            probs.astype(jnp.bfloat16),
            value_piece,
            preferred_element_type=jnp.float32,
        )
        accum = update
        return (new_peak, totals, accum)

    peak, totals, accum = lax.cond(
        jnp.int32(0) <= last_query,
        compute,
        lambda state: state,
        (peak_init, total_init, accum_init),
    )
    attended = jnp.transpose(accum / totals[..., None], (0, 3, 1, 2, 4)).astype(jnp.bfloat16)
    attended = attended.reshape(1, tok_rows, kv_local * group_size * head_dim)
    partial_sum = jnp.dot(
        attended[0], out_full.reshape(-1, width), preferred_element_type=jnp.float32
    )[None]
    head_total = lax.psum_scatter(
        partial_sum.astype(jnp.bfloat16), "exp", scatter_dimension=1, tiled=True
    ).astype(jnp.float32)
    rows = head_total.shape[1]
    own_tokens = lax.dynamic_slice_in_dim(tokens, lax.axis_index("exp") * rows, rows, 1)
    mixed = (own_tokens[0].astype(jnp.float32) + head_total[0]).astype(jnp.bfloat16)
    normed_mid = rms_norm(mixed, norm_mid)
    expert_count = w_router.shape[1]
    logits = jnp.dot(normed_mid, w_router, preferred_element_type=jnp.float32)
    choice_ids = expert_ids[0]
    picks = choice_ids[:, :, None] == jnp.arange(expert_count, dtype=jnp.int32)[None, None, :]
    chosen = jnp.sum(jnp.where(picks, logits[:, None, :], 0.0), axis=-1)
    gate_first = 1.0 / (1.0 + jnp.exp(chosen[:, 1] - chosen[:, 0]))
    gate_second = 1.0 - gate_first
    capacity = 6 * (rows // 16)
    exp_count = lax.axis_size("exp")
    exp_local = gate_up_all.shape[0]
    flat_index = choice_ids * capacity + slot_index[0]
    slot_cols = jnp.arange(expert_count * capacity, dtype=jnp.int32)
    placer = jnp.logical_or(
        slot_cols[:, None] == flat_index[None, :, 0], slot_cols[:, None] == flat_index[None, :, 1]
    ).astype(jnp.bfloat16)
    buffer_rows = jnp.dot(placer, normed_mid, preferred_element_type=jnp.float32).astype(
        jnp.bfloat16
    )
    buffer_rows = buffer_rows.reshape(exp_count, exp_local, capacity, width)
    received = lax.all_to_all(buffer_rows, "exp", split_axis=0, concat_axis=0, tiled=True)
    gathered_rows = lax.all_gather(received[None], "ctx", axis=0, tiled=True)
    gate_up_vals = jnp.einsum(
        "cnlrd,ldjf->cnlrjf", gathered_rows, gate_up_all, preferred_element_type=jnp.float32
    )
    hidden = (jax.nn.silu(gate_up_vals[..., 0, :]) * gate_up_vals[..., 1, :]).astype(jnp.bfloat16)
    summed_result = lax.psum_scatter(
        jnp.einsum("cnlrf,lfd->cnlrd", hidden, down_all, preferred_element_type=jnp.float32).astype(
            jnp.bfloat16
        ),
        "ctx",
        scatter_dimension=0,
        tiled=True,
    ).astype(jnp.float32)
    expert_out = summed_result[0].astype(jnp.bfloat16)
    returned = lax.all_to_all(expert_out, "exp", split_axis=0, concat_axis=0, tiled=True)
    returned = returned.reshape(expert_count * capacity, width)
    combiner = gate_first[:, None] * (flat_index[:, 0:1] == slot_cols[None, :]).astype(
        jnp.float32
    ) + gate_second[:, None] * (flat_index[:, 1:2] == slot_cols[None, :]).astype(jnp.float32)
    moe_total = jnp.dot(combiner, returned.astype(jnp.float32), precision=lax.Precision.HIGHEST)
    return (mixed.astype(jnp.float32) + moe_total).astype(jnp.bfloat16)[None]


def solution(mesh):
    placed = (
        P("dp", "ctx", None),
        P(),
        P("dp", "exp", None, None),
        P("exp", None, None, "dp"),
        P(),
        P(),
        P("exp", "dp", None, "ctx"),
        P("exp", "ctx", "dp"),
        P("dp", ("ctx", "exp"), None),
        P("dp", ("ctx", "exp"), None),
    )
    return jax.shard_map(
        on_device,
        mesh=mesh,
        in_specs=placed,
        out_specs=P("dp", ("ctx", "exp"), None),
        check_vma=False,
    )
```

profile of v0, /device:TPU:2, one launch (start us, length us, event | category | flops | bytes accessed | tf_op | source)
XLA Modules:
  0.0 595.8 jit_solution(7468417833645752006)
XLA Ops:
  6.5 4.8 copy.44
  11.3 0.0 all-gather.8.cloned.1.call-update
  11.3 0.0 all-gather.10.cloned.1.call-start
  11.4 0.7 all-gather.10.cloned.1.call-update
  12.1 0.0 reduce-scatter.3.cloned.1.call-start
  12.2 0.4 copy-done.1
  12.6 0.3 fusion.27
  12.8 0.2 multiply_cosine_fusion
  13.1 86.9 %all-gather.8.cloned.1.call-done = bf16[4096,1,6,128]{0,3,2,1:T(8,128)(2,1)} async-done(((bf16[2048,1,6,128]{0,3,2,1:T(8,128)(2,1)}), bf16[4096,1,6,128]{0,3,2,1:T(8,128)(2,1)}) %all-gather.8.cloned.1.call-update) | async-done | bytes 6291472 | tf_op jit(solution)/shard_map/all_gather | solution.py:48
  99.9 4.6 fusion.36
  104.6 0.2 fusion.54
  104.9 21.1 %all_gather.22 = bf16[1,2048,1,128]{1,3,2,0:T(8,128)(2,1)S(1)} all-gather(bf16[1,128,1,128]{1,3,2,0:T(8,128)(2,1)S(1)} %pad_maximum_fusion.1), channel_id=1, replica_groups=mesh['ctx'=16,'exp'=8,'dp'=2] {'ctx'}, dimensions={1}, use_global_device_ids=true | all-gather | bytes 557056 | tf_op jit(solution)/shard_map/all_gather | solution.py:71
  126.0 25.5 %all-gather = bf16[1,2048,1,1,128]{1,4,3,2,0:T(8,128)(2,1)S(1)} all-gather(bf16[1,128,1,1,128]{1,4,3,2,0:T(8,128)(2,1)S(1)} %slice.86), channel_id=2, replica_groups=mesh['ctx'=16,'exp'=8,'dp'=2] {'ctx'}, dimensions={1}, use_global_device_ids=true | all-gather | bytes 557056 | tf_op jit(solution)/shard_map/all_gather | solution.py:72
  151.4 3.1 conditional.1
  151.4 0.2 iota_compare_fusion
  151.6 0.8 fusion
  152.4 1.1 fusion.7
  153.5 1.0 fusion.2
  154.5 10.0 %all-gather.10.cloned.1.call-done = bf16[1,4,128,4096]{3,2,1,0:T(8,128)(2,1)} async-done(((bf16[1,4,128,2048]{3,2,1,0:T(8,128)(2,1)}), bf16[1,4,128,4096]{3,2,1,0:T(8,128)(2,1)}) %all-gather.10.cloned.1.call-update) | async-done | bytes 4194320 | tf_op jit(solution)/shard_map/all_gather | solution.py:49
  164.6 3.9 fusion.23
  168.5 0.0 reduce-scatter.3.cloned.1.call-update
  168.5 0.0 all-gather.12.cloned.1.call-start
  168.6 4.9 copy.51
  173.5 0.0 all-gather.16.cloned.1.call-start
  173.5 0.6 copy-done.3
  174.2 36.3 %reduce-scatter.3.cloned.1.call-done = bf16[1,16,4096]{2,1,0:T(8,128)(2,1)} async-done(((bf16[1,128,4096]{2,1,0:T(8,128)(2,1)}), bf16[1,16,4096]{2,1,0:T(8,128)(2,1)}) %reduce-scatter.3.cloned.1.call-update) | async-done | bytes 131088 | tf_op jit(solution)/shard_map/reduce_scatter | solution.py:107
  210.5 1.1 fusion.45
  211.6 0.3 convolution_convert_fusion.2
  211.9 0.1 reshape.364
  212.0 17.6 %all_to_all.10 = bf16[8,1,6,4096]{3,2,1,0:T(8,128)(2,1)S(1)} all-to-all(bf16[8,1,6,4096]{3,2,1,0:T(8,128)(2,1)S(1)} %bitcast.132), channel_id=1, replica_groups=mesh['ctx'=16,'exp'=8,'dp'=2] {'exp'}, dimensions={0} | all-to-all | bytes 786432 | tf_op jit(solution)/shard_map/all_to_all | solution.py:133
  229.6 1.0 copy.50
  230.6 0.0 all-gather.16.cloned.1.call-update
  230.6 0.0 all-gather.14.cloned.1.call-start
  230.7 0.5 all-gather.14.cloned.1.call-update
  231.2 0.2 reduce-scatter.5.cloned.1.call-start
  231.4 88.6 %all-gather.12.cloned.1.call-done = bf16[1,4096,2,512]{3,1,2,0:T(8,128)(2,1)} async-done(((bf16[1,2048,2,512]{3,1,2,0:T(8,128)(2,1)}), bf16[1,4096,2,512]{3,1,2,0:T(8,128)(2,1)}) %all-gather.12.cloned.1.call-update) | async-done | bytes 8388624 | tf_op jit(solution)/shard_map/all_gather | solution.py:50
  320.0 72.3 %all-gather.16.cloned.1.call-done = bf16[128,1,6,4096]{3,0,2,1:T(8,128)(2,1)} async-done(((bf16[8,1,6,4096]{3,0,2,1:T(8,128)(2,1)}), bf16[128,1,6,4096]{3,0,2,1:T(8,128)(2,1)}) %all-gather.16.cloned.1.call-update) | async-done | bytes 6291472 | tf_op jit(solution)/shard_map/all_gather | solution.py:134
  392.3 12.1 %fusion.30 = f32[16,8,1,6,2,512]{5,1,4,3,0,2:T(8,128)} fusion(bf16[1,4096,2,512]{3,1,2,0:T(8,128)(2,1)} %all-gather.12.cloned.1.call-done, bf16[128,1,6,4096]{3,0,2,1:T(8,128)(2,1)} %all-gather.16.cloned.1.call-done), kind=kOutput, calls=%fused_computation.38 | convolution fusion | flops 6442450944 | bytes 17825792 | tf_op jit(solution)/shard_map/cnlrd,ldjf->cnlrjf/dot_general | solution.py:135
  404.4 50.6 %all-gather.14.cloned.1.call-done = bf16[1,512,4096]{2,1,0:T(8,128)(2,1)} async-done(((bf16[1,512,2048]{2,1,0:T(8,128)(2,1)}), bf16[1,512,4096]{2,1,0:T(8,128)(2,1)}) %all-gather.14.cloned.1.call-update) | async-done | bytes 4194320 | tf_op jit(solution)/shard_map/all_gather | solution.py:51
  455.0 9.2 %fusion.22 = bf16[16,8,1,6,4096]{4,1,3,0,2:T(8,128)(2,1)} fusion(bf16[1,512,4096]{2,1,0:T(8,128)(2,1)} %all-gather.14.cloned.1.call-done, f32[16,8,1,6,2,512]{5,1,4,3,0,2:T(8,128)} %fusion.30), kind=kOutput, calls=%fused_computation.25 | convolution fusion | flops 3226730496 | bytes 13631488 | tf_op jit(solution)/shard_map/cnlrf,lfd->cnlrd/dot_general | solution.py:140
  464.2 0.0 reduce-scatter.5.cloned.1.call-update
  464.3 98.2 %reduce-scatter.5.cloned.1.call-done = bf16[1,8,1,6,4096]{4,1,3,0,2:T(8,128)(2,1)} async-done(((bf16[16,8,1,6,4096]{4,1,3,0,2:T(8,128)(2,1)}), bf16[1,8,1,6,4096]{4,1,3,0,2:T(8,128)(2,1)}) %reduce-scatter.5.cloned.1.call-update) | async-done | bytes 393232 | tf_op jit(solution)/shard_map/reduce_scatter | solution.py:139
  562.5 2.0 copy.53
  564.5 7.0 %all-to-all-start.1 = ((bf16[8,1,6,4096]{3,2,1,0:T(8,128)(2,1)}), bf16[8,1,6,4096]{3,2,1,0:T(8,128)(2,1)S(1)}, u32[]{:S(2)}, u32[]{:S(2)}) async-start(bf16[8,1,6,4096]{3,2,1,0:T(8,128)(2,1)} %copy.53), calls=%async_computation.3 | async-start | bytes 1048576 | tf_op jit(solution)/shard_map/all_to_all | solution.py:148
  571.5 0.2 fusion.58
  571.8 16.1 %all-to-all-done.1 = bf16[8,1,6,4096]{3,2,1,0:T(8,128)(2,1)S(1)} async-done(((bf16[8,1,6,4096]{3,2,1,0:T(8,128)(2,1)}), bf16[8,1,6,4096]{3,2,1,0:T(8,128)(2,1)S(1)}, u32[]{:S(2)}, u32[]{:S(2)}) %all-to-all-start.1) | async-done | bytes 393248 | tf_op jit(solution)/shard_map/all_to_all | solution.py:148
  587.8 0.1 reshape.368
  588.0 1.0 fusion.25
  (31 shorter events, 0.2 us)
Async XLA Ops:
  6.5 565.0 %copy-start = (bf16[4096,8]{0,1:T(8,128)(2,1)S(1)}, bf16[4096,8]{0,1:T(8,128)(2,1)}, u32[]{:S(2)}) copy-start(bf16[4096,8]{0,1:T(8,128)(2,1)} %param.17) | copy-start | bytes 196612
  6.5 93.4 %all-gather.8.cloned.1.call-start = ((), (), s32[]{:S(2)}) async-start(), calls=%async_computation.4 | async-start | bytes 9437184 | tf_op jit(solution)/shard_map/all_gather | solution.py:48
  11.3 0.8 copy-start.2
  11.3 1.2 copy-start.1
  11.3 153.2 %all-gather.10.cloned.1.call-start = ((), (), s32[]{:S(2)}) async-start(), calls=%async_computation.5 | async-start | bytes 6291456 | tf_op jit(solution)/shard_map/all_gather | solution.py:49
  12.1 198.4 %reduce-scatter.3.cloned.1.call-start = ((), (), s32[]{:S(2)}) async-start(), calls=%async_computation.6 | async-start | bytes 1179648 | tf_op jit(solution)/shard_map/reduce_scatter | solution.py:107
  168.5 151.5 %all-gather.12.cloned.1.call-start = ((), (), s32[]{:S(2)}) async-start(), calls=%async_computation.7 | async-start | bytes 12582912 | tf_op jit(solution)/shard_map/all_gather | solution.py:50
  173.5 0.7 copy-start.3
  173.5 0.7 copy-start.4
  173.5 0.7 copy-start.5
  173.5 218.9 %all-gather.16.cloned.1.call-start = ((), (), s32[]{:S(2)}) async-start(), calls=%async_computation.10 | async-start | bytes 6684672 | tf_op jit(solution)/shard_map/all_gather | solution.py:134
  230.6 224.4 %all-gather.14.cloned.1.call-start = ((), (), s32[]{:S(2)}) async-start(), calls=%async_computation.8 | async-start | bytes 6291456 | tf_op jit(solution)/shard_map/all_gather | solution.py:51
  231.2 331.3 %reduce-scatter.5.cloned.1.call-start = ((), (), s32[]{:S(2)}) async-start(), calls=%async_computation.9 | async-start | bytes 6684672 | tf_op jit(solution)/shard_map/reduce_scatter | solution.py:139
  564.5 23.4 %all-to-all-start.1 = ((bf16[8,1,6,4096]{3,2,1,0:T(8,128)(2,1)}), bf16[8,1,6,4096]{3,2,1,0:T(8,128)(2,1)S(1)}, u32[]{:S(2)}, u32[]{:S(2)}) async-start(bf16[8,1,6,4096]{3,2,1,0:T(8,128)(2,1)} %copy.53), calls=%async_computation.3 | async-start | bytes 1048576 | tf_op jit(solution)/shard_map/all_to_all | solution.py:148
Sparse Core Ops, SparseCore 0:
  11.5 88.4 all-gather.7
  101.7 62.8 all-gather.9
  168.6 41.8 reduce-scatter.2
  212.2 107.8 all-gather.11
  322.7 69.6 all-gather.15
  394.0 60.9 all-gather.13
  464.4 98.0 reduce-scatter.4
where the time goes:
time: 596 us
  waiting for transfers between devices  460 us (77%)
  blocking collectives  64.1 us (11%)
  matrix products  33.3 us (6%)
  local copies, waits for them, and re-layouts  14 us (2%)
  between operations  13.7 us (2%)
  starting transfers between devices  7.44 us (1%)
    reduce_scatter x1, waiting for transfers between devices, on_device(): lax.psum_scatter(jnp.einsum('cnlrf,lfd->cnlrd', hidden, down_all, preferr...  98.2 us
    all_gather x1, waiting for transfers between devices, on_device(): lax.all_gather(w_gate_up, 'dp', axis=1, tiled=True)  88.6 us
    all_gather x1, waiting for transfers between devices, on_device(): lax.all_gather(w_qkv, 'dp', axis=0, tiled=True)  86.9 us
    all_gather x1, waiting for transfers between devices, on_device(): gathered_rows = lax.all_gather(received[None], 'ctx', axis=0, tiled=True)  72.3 us
    all_gather x1, waiting for transfers between devices, on_device(): lax.all_gather(w_down, 'dp', axis=2, tiled=True)  50.6 us
    reduce_scatter x1, waiting for transfers between devices, on_device(): lax.psum_scatter(partial_sum.astype(jnp.bfloat16), 'exp', scatter_dimensi...  36.3 us
    all_gather x1, blocking collectives, on_device(): value_piece = lax.all_gather(values, 'ctx', axis=1, tiled=True)  25.5 us
    all_gather x1, blocking collectives, on_device(): key_piece = lax.all_gather(keys_rot, 'ctx', axis=1, tiled=True)  21.1 us
  transfers between devices with their start and end apart: 8, of which 8 were waited for; matrix products, arithmetic and copies ran while one was open for 5% of the time, Pallas kernels for 0%

commit v1 on v0

v1 whole, which is shorter than its diff:
```python
import math

import jax
import jax.numpy as jnp
from jax import lax
from jax.sharding import Mesh
from jax.sharding import PartitionSpec as P

EPSILON = 1e-05
ROPE_BASE = 1000000.0
F32 = jnp.float32
BF16 = jnp.bfloat16
SWAP = [(0, 1), (1, 0)]
CHIPS = ("yh", "x")


def rope_angles(positions, head_dim):
    half_dim = head_dim // 2
    freqs = jnp.exp(jnp.arange(half_dim, dtype=F32) * (-2.0 * math.log(ROPE_BASE) / head_dim))
    return positions[:, None] * freqs[None, :]


def rotate(tensor, angles):
    half_dim = tensor.shape[-1] // 2
    first_half = tensor[..., :half_dim]
    second_half = tensor[..., half_dim:]
    cosine = jnp.cos(angles)
    sine = jnp.sin(angles)
    return jnp.concatenate(
        [first_half * cosine - second_half * sine, second_half * cosine + first_half * sine],
        axis=-1,
    )


def swap_dp(array):
    return lax.ppermute(array, "dp", SWAP)


def swap_core(array):
    return lax.ppermute(array, "core", SWAP)


def forward_pairs(step_y, step_x):
    return [
        (y * 4 + x, (y ^ step_y) * 4 + (x + step_x) % 4) for y in range(2) for x in range(4)
    ]


def backward_pairs(step_y, step_x):
    return [(b, a) for a, b in forward_pairs(step_y, step_x)]


STEPS = [(0, 0), (1, 0), (0, 1), (0, 3), (1, 1), (1, 3), (0, 2), (1, 2)]


def halves(array, part):
    size = array.shape[-1] // 2
    own = lax.dynamic_slice_in_dim(array, part * size, size, array.ndim - 1)
    other = lax.dynamic_slice_in_dim(array, (1 - part) * size, size, array.ndim - 1)
    return own, other


def on_device(
    tokens, norm_in, w_qkv, w_out, norm_mid, w_router, w_gate_up, w_down, expert_ids, slot_index
):
    part = lax.axis_index("dp")
    core = lax.axis_index("core")
    chip = lax.axis_index("yh") * 4 + lax.axis_index("x")
    tok_rows = tokens.shape[1]
    width = tokens.shape[2]
    half = width // 2
    head_dim = w_qkv.shape[3]
    group_size = w_qkv.shape[2] - 2

    wide = tokens[0].astype(F32)
    scale_in = lax.rsqrt(jnp.mean(wide * wide, axis=-1, keepdims=True) + EPSILON)
    normed = (wide * scale_in * norm_in.astype(F32)).astype(BF16)
    normed_own, normed_other = halves(normed, part)
    normed_peer = swap_dp(normed_other)
    weights_in = w_qkv.reshape(half, -1)
    to_peer = jnp.dot(normed_peer, weights_in, preferred_element_type=F32).astype(BF16)
    from_peer = swap_dp(to_peer)
    projected = jnp.dot(normed_own, weights_in, preferred_element_type=F32) + from_peer.astype(F32)
    projected = projected.reshape(tok_rows, group_size + 2, head_dim)

    gate_up_own, down_own, _ = lax.optimization_barrier((w_gate_up[0], w_down[0], from_peer))
    gate_up_other = swap_dp(gate_up_own)
    down_other = swap_dp(down_own)

    query_idx = (chip * 2 + core) * tok_rows + jnp.arange(tok_rows, dtype=jnp.int32)
    angles = rope_angles(query_idx.astype(F32), head_dim)
    queries = rotate(projected[:, :group_size], angles[:, None, :]).astype(BF16)
    keys_rot = rotate(projected[:, group_size], angles).astype(BF16)
    values = projected[:, group_size + 1].astype(BF16)

    keys_values = jnp.concatenate([keys_rot, values], axis=-1)
    pieces = [keys_values] + [
        lax.ppermute(keys_values, CHIPS, [(i, i + step) for i in range(8 - step)])
        for step in range(1, 8)
    ]
    same_core = jnp.stack(pieces)
    all_pieces = jnp.stack([same_core, swap_core(same_core)])
    step_idx = jnp.arange(8, dtype=jnp.int32)[None, :, None]
    parity = jnp.stack([core, 1 - core])[:, None, None]
    key_idx = (
        ((chip - step_idx) * 2 + parity) * tok_rows
        + jnp.arange(tok_rows, dtype=jnp.int32)[None, None, :]
    ).reshape(-1)
    count = key_idx.shape[0]
    all_keys = all_pieces[..., :head_dim].reshape(count, head_dim)
    all_values = all_pieces[..., head_dim:].reshape(count, head_dim)
    scores = jnp.einsum("qgd,sd->gqs", queries, all_keys, preferred_element_type=F32) * (
        1.0 / math.sqrt(head_dim)
    )
    causal = jnp.logical_and(key_idx[None, :] <= query_idx[:, None], key_idx[None, :] >= 0)
    scores = jnp.where(causal, scores, -1e30)
    peak = jnp.max(scores, axis=-1, keepdims=True)
    probs = jnp.where(causal, jnp.exp(scores - peak), 0.0)
    totals = jnp.sum(probs, axis=-1)
    accum = jnp.einsum("gqs,sd->gqd", probs.astype(BF16), all_values, preferred_element_type=F32)
    attended = jnp.transpose(accum / totals[..., None], (1, 0, 2)).astype(BF16)
    attended = attended.reshape(tok_rows, group_size * head_dim)

    both = jnp.stack([attended, swap_dp(attended)])
    partial_sum = jnp.einsum(
        "bth,hd->btd", both, w_out.reshape(-1, half), preferred_element_type=F32
    ).astype(BF16)
    summed = lax.psum_scatter(partial_sum, "exp", scatter_dimension=1, tiled=True)
    rows = summed.shape[1]
    head_total = jnp.concatenate([summed[0], swap_dp(summed[1])], axis=-1).astype(F32)
    own_tokens = lax.dynamic_slice_in_dim(tokens[0], lax.axis_index("exp") * rows, rows, 0)
    own_tokens = jnp.concatenate(halves(own_tokens, part), axis=-1)
    mixed = (own_tokens.astype(F32) + head_total).astype(BF16)

    wide_mid = mixed.astype(F32)
    scale_mid = lax.rsqrt(jnp.mean(wide_mid * wide_mid, axis=-1, keepdims=True) + EPSILON)
    gain_mid = jnp.concatenate(halves(norm_mid, part), axis=-1).astype(F32)
    normed_mid = (wide_mid * scale_mid * gain_mid).astype(BF16)
    router = jnp.concatenate(
        [
            lax.dynamic_slice_in_dim(w_router, part * half, half, 0),
            lax.dynamic_slice_in_dim(w_router, (1 - part) * half, half, 0),
        ],
        axis=0,
    )
    logits = jnp.dot(normed_mid, router, preferred_element_type=F32)
    expert_count = w_router.shape[1]
    choice_ids = expert_ids[0]
    picks = choice_ids[:, :, None] == jnp.arange(expert_count, dtype=jnp.int32)[None, None, :]
    chosen = jnp.sum(jnp.where(picks, logits[:, None, :], 0.0), axis=-1)
    gate_first = 1.0 / (1.0 + jnp.exp(chosen[:, 1] - chosen[:, 0]))
    gate_second = 1.0 - gate_first
    capacity = 6
    flat_index = choice_ids * capacity + slot_index[0]
    slot_cols = jnp.arange(expert_count * capacity, dtype=jnp.int32)
    placer = jnp.logical_or(
        slot_cols[:, None] == flat_index[None, :, 0], slot_cols[:, None] == flat_index[None, :, 1]
    ).astype(BF16)
    buffer_rows = jnp.dot(placer, normed_mid, preferred_element_type=F32).astype(BF16)
    buffer_rows = buffer_rows.reshape(expert_count, capacity, width)
    received = lax.all_to_all(buffer_rows, "exp", split_axis=0, concat_axis=0, tiled=True)
    received = received.reshape(expert_count * capacity, width)

    same_core_rows = jnp.stack(
        [received] + [lax.ppermute(received, CHIPS, forward_pairs(*s)) for s in STEPS[1:]]
    )
    expert_rows = jnp.stack([same_core_rows, swap_core(same_core_rows)]).reshape(-1, width)
    gate_up = jnp.einsum(
        "rd,djf->rjf", expert_rows[:, :half], gate_up_own, preferred_element_type=F32
    ) + jnp.einsum("rd,djf->rjf", expert_rows[:, half:], gate_up_other, preferred_element_type=F32)
    hidden = (jax.nn.silu(gate_up[:, 0]) * gate_up[:, 1]).astype(BF16)
    down = jnp.concatenate(
        [
            jnp.dot(hidden, down_own, preferred_element_type=F32).astype(BF16),
            jnp.dot(hidden, down_other, preferred_element_type=F32).astype(BF16),
        ],
        axis=-1,
    ).reshape(2, 8, expert_count * capacity, width)

    pair_sum = (down[0].astype(F32) + swap_core(down[1]).astype(F32)).astype(BF16)
    total = pair_sum[0].astype(F32)
    for index, step in enumerate(STEPS[1:]):
        total = total + lax.ppermute(pair_sum[index + 1], CHIPS, backward_pairs(*step)).astype(F32)
    expert_out = total.astype(BF16).reshape(expert_count, capacity, width)
    returned = lax.all_to_all(expert_out, "exp", split_axis=0, concat_axis=0, tiled=True)
    returned = returned.reshape(expert_count * capacity, width)
    combiner = gate_first[:, None] * (flat_index[:, 0:1] == slot_cols[None, :]).astype(
        F32
    ) + gate_second[:, None] * (flat_index[:, 1:2] == slot_cols[None, :]).astype(F32)
    moe_total = jnp.dot(combiner, returned.astype(F32), precision=lax.Precision.HIGHEST)
    layer_out = (mixed.astype(F32) + moe_total).astype(BF16)
    return jnp.concatenate(halves(layer_out, part), axis=-1)[None]


def solution(mesh):
    fine = Mesh(mesh.devices.reshape(2, 4, 2, 8, 2), ("yh", "x", "core", "exp", "dp"))
    ctx = ("yh", "x", "core")
    rows = ctx + ("exp",)
    placed = (
        P("dp", ctx, None),
        P(),
        P("dp", "exp", None, None),
        P("exp", None, None, "dp"),
        P(),
        P(),
        P("exp", "dp", None, ctx),
        P("exp", ctx, "dp"),
        P("dp", rows, None),
        P("dp", rows, None),
    )
    return jax.shard_map(
        on_device,
        mesh=fine,
        in_specs=placed,
        out_specs=P("dp", rows, None),
        check_vma=False,
    )
```

time: 596 us -> 411 us (0.69)
  waiting for transfers between devices: 460 us -> 265 us
  blocking collectives: 64.1 us -> 0 us
  starting transfers between devices: 7.44 us -> 65.4 us
  other arithmetic: 3.13 us -> 15.7 us
    all_gather x5 -> x0, waiting for transfers between devices: 308 us -> none  [the longest x1 88.6 us: on_device(): lax.all_gather(w_gate_up, 'dp', axis=1, tiled=True)]
    ppermute x0 -> x30, waiting for transfers between devices: none -> 198 us  [the longest x7 108 us: on_device(): lax.ppermute(received, CHIPS, forward_pairs(*s))]
    reduce_scatter x2 -> x1, waiting for transfers between devices: 135 us -> 42.9 us  [on_device(): lax.psum_scatter(partial_sum, 'exp', scatter_dimension=1, tiled=True)]
    ppermute x0 -> x30, starting transfers between devices: none -> 52.1 us  [the longest x7 17.7 us: on_device(): lax.ppermute(keys_values, CHIPS, [(i, i + step) for i in range(8 - step)])]
    all_gather x2 -> x0, blocking collectives: 46.6 us -> none  [the longest x1 25.5 us: on_device(): value_piece = lax.all_gather(values, 'ctx', axis=1, tiled=True)]
    all_to_all x1 -> x0, blocking collectives: 17.6 us -> none  [on_device(): lax.all_to_all(buffer_rows, 'exp', split_axis=0, concat_axis=0, tiled=True)]
    all_to_all x0 -> x1, waiting for transfers between devices: none -> 6.98 us  [on_device(): lax.all_to_all(buffer_rows, 'exp', split_axis=0, concat_axis=0, tiled=True)]
    dot_general x9 -> x11, matrix products: 33.3 us -> 27.5 us  [the longest x1 5.42 us: on_device(): jnp.einsum('rd,djf->rjf', expert_rows[:, :half], gate_up_own, preferred_e...]
  transfers between devices with their start and end apart: 8 -> 33, of which waited for: 8 -> 20; matrix products, arithmetic and copies ran while one was open for 5% -> 8% of each run, Pallas kernels for 0% -> 0%
where the time goes in v1:
time: 411 us; the launch traced here: 407 us
  waiting for transfers between devices  265 us (64%)
  starting transfers between devices  65.4 us (16%)
  matrix products  30.7 us (7%)
  local copies, waits for them, and re-layouts  16.4 us (4%)
  other arithmetic  15.7 us (4%)
  between operations  14 us (3%)
    ppermute x7, waiting for transfers between devices, on_device(): lax.ppermute(received, CHIPS, forward_pairs(*s))  108 us
    ppermute x6, waiting for transfers between devices, swap_dp(): return lax.ppermute(array, 'dp', SWAP)  45.9 us
    reduce_scatter x1, waiting for transfers between devices, on_device(): lax.psum_scatter(partial_sum, 'exp', scatter_dimension=1, tiled=True)  42.9 us
    ppermute x7, waiting for transfers between devices, on_device(): lax.ppermute(pair_sum[index + 1], CHIPS, backward_pairs(*step)).astype(F32)  32.1 us
    ppermute x7, starting transfers between devices, on_device(): lax.ppermute(keys_values, CHIPS, [(i, i + step) for i in range(8 - step)])  17.7 us
    all_to_all x1, waiting for transfers between devices, on_device(): lax.all_to_all(expert_out, 'exp', split_axis=0, concat_axis=0, tiled=True)  17 us
    ppermute x7, starting transfers between devices, on_device(): lax.ppermute(pair_sum[index + 1], CHIPS, backward_pairs(*step)).astype(F32)  13.3 us
    ppermute x7, starting transfers between devices, on_device(): lax.ppermute(received, CHIPS, forward_pairs(*s))  13.2 us
  transfers between devices with their start and end apart: 33, of which 20 were waited for; matrix products, arithmetic and copies ran while one was open for 8% of the time, Pallas kernels for 0%

profile of v1, /device:TPU:2, one launch (start us, length us, event | category | flops | bytes accessed | tf_op | source)
XLA Modules:
  0.0 407.1 jit_solution(18351911722099054209)
XLA Ops:
  7.4 1.5 fusion.7
  8.9 1.6 fusion.9
  11.3 1.6 collective-permute-start
  13.4 4.7 %copy.37 = bf16[2048,1,6,128]{0,3,2,1:T(8,128)(2,1)} copy(bf16[2048,1,6,128]{3,0,2,1:T(8,128)(2,1)} %param.12) | data formatting | bytes 6291456 | tf_op args[2]
  18.8 6.5 %collective-permute-done = bf16[128,2048]{1,0:T(8,128)(2,1)} collective-permute-done((bf16[128,2048]{1,0:T(8,128)(2,1)}, bf16[128,2048]{1,0:T(8,128)(2,1)}, u32[]{:S(2)}, u32[]{:S(2)}) %collective-permute-start) | collective-permute-done | bytes 524320 | tf_op jit(solution)/shard_map/ppermute | solution.py:36
  25.3 3.2 convolution_convert_fusion.4
  28.5 1.7 collective-permute-start.1
  30.3 4.1 %collective-permute-done.1 = bf16[128,768]{1,0:T(8,128)(2,1)S(1)} collective-permute-done((bf16[128,768]{1,0:T(8,128)(2,1)S(1)}, bf16[128,768]{1,0:T(8,128)(2,1)S(1)}, u32[]{:S(2)}, u32[]{:S(2)}) %collective-permute-start.1) | collective-permute-done | bytes 196640 | tf_op jit(solution)/shard_map/ppermute | solution.py:36
  37.1 3.4 collective-permute-start.2
  40.6 5.6 %collective-permute-start.3 = (bf16[128,256]{1,0:T(8,128)(2,1)S(1)}, bf16[128,256]{1,0:T(8,128)(2,1)S(1)}, u32[]{:S(2)}, u32[]{:S(2)}) collective-permute-start(bf16[128,256]{1,0:T(8,128)(2,1)S(1)} %get-tuple-element.14), channel_id=1, source_target_pairs={{0,64},{32,96},{64,128},{96,160},{128,192},{160,224},{1,65},{33,97... | collective-permute-start | bytes 196616 | tf_op jit(solution)/shard_map/ppermute | solution.py:98
  46.3 4.1 collective-permute-start.4
  56.3 2.3 compare_and_fusion
  59.8 2.1 pad_maximum_fusion.2
  61.9 3.1 fusion.80
  65.0 3.0 fusion.24
  69.0 5.1 %collective-permute-done.10 = bf16[128,512]{1,0:T(8,128)(2,1)S(1)} collective-permute-done((bf16[128,512]{1,0:T(8,128)(2,1)S(1)}, bf16[128,512]{1,0:T(8,128)(2,1)S(1)}, u32[]{:S(2)}, u32[]{:S(2)}) %collective-permute-start.10) | collective-permute-done | bytes 131104 | tf_op jit(solution)/shard_map/ppermute | solution.py:36
  74.1 1.7 convolution_convert_fusion.3
  77.0 42.9 %reduce-scatter.2.cloned.1.call-done = bf16[2,16,2048]{2,1,0:T(8,128)(2,1)} async-done(((bf16[2,128,2048]{2,1,0:T(8,128)(2,1)}), bf16[2,16,2048]{2,1,0:T(8,128)(2,1)}) %reduce-scatter.2.cloned.1.call-update) | async-done | bytes 131088 | tf_op jit(solution)/shard_map/reduce_scatter | solution.py:128
  120.9 1.7 collective-permute-start.11
  122.6 2.8 collective-permute-done.11
  126.9 4.5 %all-to-all-start = ((bf16[8,6,4096]{2,1,0:T(8,128)(2,1)}), bf16[8,6,4096]{2,1,0:T(8,128)(2,1)S(1)}, u32[]{:S(2)}, u32[]{:S(2)}) async-start(bf16[8,6,4096]{2,1,0:T(8,128)(2,1)} %reshape.220), calls=%async_computation.1 | async-start | bytes 1048576 | tf_op jit(solution)/shard_map/all_to_all | solution.py:161
  131.4 4.8 %copy.56 = bf16[1,2048,2,512]{3,1,2,0:T(8,128)(2,1)} copy(bf16[1,2048,2,512]{3,2,1,0:T(2,128)(2,1)} %param.16) | data formatting | bytes 8388608 | tf_op args[6]
  137.8 7.0 %all-to-all-done = bf16[8,6,4096]{2,1,0:T(8,128)(2,1)S(1)} async-done(((bf16[8,6,4096]{2,1,0:T(8,128)(2,1)}), bf16[8,6,4096]{2,1,0:T(8,128)(2,1)S(1)}, u32[]{:S(2)}, u32[]{:S(2)}) %all-to-all-start) | async-done | bytes 393248 | tf_op jit(solution)/shard_map/all_to_all | solution.py:161
  144.9 3.1 collective-permute-start.12
  151.6 94.9 %collective-permute-done.12 = bf16[48,4096]{1,0:T(8,128)(2,1)S(1)} collective-permute-done((bf16[48,4096]{1,0:T(8,128)(2,1)S(1)}, bf16[48,4096]{1,0:T(8,128)(2,1)S(1)}, u32[]{:S(2)}, u32[]{:S(2)}) %collective-permute-start.12) | collective-permute-done | bytes 393248 | tf_op jit(solution)/shard_map/ppermute | solution.py:165
  247.3 2.5 collective-permute-start.17
  249.8 3.4 collective-permute-start.18
  253.3 4.9 %collective-permute-done.16 = bf16[48,4096]{1,0:T(8,128)(2,1)S(1)} collective-permute-done((bf16[48,4096]{1,0:T(8,128)(2,1)S(1)}, bf16[48,4096]{1,0:T(8,128)(2,1)S(1)}, u32[]{:S(2)}, u32[]{:S(2)}) %collective-permute-start.16) | collective-permute-done | bytes 393248 | tf_op jit(solution)/shard_map/ppermute | solution.py:165
  258.2 2.0 collective-permute-done.17
  260.2 6.4 %collective-permute-done.18 = bf16[48,4096]{1,0:T(8,128)(2,1)S(1)} collective-permute-done((bf16[48,4096]{1,0:T(8,128)(2,1)S(1)}, bf16[48,4096]{1,0:T(8,128)(2,1)S(1)}, u32[]{:S(2)}, u32[]{:S(2)}) %collective-permute-start.18) | collective-permute-done | bytes 393248 | tf_op jit(solution)/shard_map/ppermute | solution.py:165
  267.3 5.1 %collective-permute-done.19 = bf16[8,48,4096]{2,1,0:T(8,128)(2,1)S(1)} collective-permute-done((bf16[8,48,4096]{2,1,0:T(8,128)(2,1)S(1)}, bf16[8,48,4096]{2,1,0:T(8,128)(2,1)S(1)}, u32[]{:S(2)}, u32[]{:S(2)}) %collective-permute-start.19) | collective-permute-done | bytes 3145760 | tf_op jit(solution)/shard_map/ppermute | solution.py:40
  273.0 5.4 %fusion.5 = f32[768,2,512]{2,0,1:T(8,128)S(1)} fusion(bf16[2048,2,512]{2,0,1:T(8,128)(2,1)} %collective-permute-done.20, bf16[768,4096]{1,0:T(8,128)(2,1)S(1)} %bitcast.164), kind=kOutput, calls=%fused_computation.18 | convolution fusion | flops 3221225472 | bytes 10485760 | tf_op jit(solution)/shard_map/rd,djf->rjf/dot_general | solution.py:170
  278.3 5.4 %fusion.15 = f32[768,2,512]{2,0,1:T(8,128)S(1)} fusion(f32[768,2,512]{2,0,1:T(8,128)S(1)} %fusion.5, bf16[2048,2,512]{2,0,1:T(8,128)(2,1)} %bitcast.159, bf16[768,4096]{1,0:T(8,128)(2,1)S(1)} %bitcast.165), kind=kOutput, calls=%fused_computation.32 | convolution fusion | flops 3222011904 | bytes 13631488 | tf_op jit(solution)/shard_map/rd,djf->rjf/dot_general | solution.py:168
  284.3 3.4 convolution_convert_fusion.2
  287.7 27.4 %collective-permute-done.21 = bf16[512,2048]{1,0:T(8,128)(2,1)} collective-permute-done((bf16[512,2048]{1,0:T(8,128)(2,1)}, bf16[512,2048]{1,0:T(8,128)(2,1)}, u32[]{:S(2)}, u32[]{:S(2)}) %collective-permute-start.21) | collective-permute-done | bytes 2097184 | tf_op jit(solution)/shard_map/ppermute | solution.py:36
  315.1 3.4 convolution_convert_fusion.1
  319.2 5.6 %collective-permute-done.22 = bf16[8,48,4096]{2,1,0:T(8,128)(2,1)S(1)} collective-permute-done((bf16[8,48,4096]{2,1,0:T(8,128)(2,1)S(1)}, bf16[8,48,4096]{2,1,0:T(8,128)(2,1)S(1)}, u32[]{:S(2)}, u32[]{:S(2)}) %collective-permute-start.22) | collective-permute-done | bytes 3145760 | tf_op jit(solution)/shard_map/ppermute | solution.py:40
  327.2 2.0 collective-permute-start.25
  329.2 3.8 collective-permute-start.26
  333.7 5.4 %collective-permute-done.23 = bf16[48,4096]{1,0:T(8,128)(2,1)S(1)} collective-permute-done((bf16[48,4096]{1,0:T(8,128)(2,1)S(1)}, bf16[48,4096]{1,0:T(8,128)(2,1)S(1)}, u32[]{:S(2)}, u32[]{:S(2)}) %collective-permute-start.23) | collective-permute-done | bytes 393248 | tf_op jit(solution)/shard_map/ppermute | solution.py:183
  339.1 2.5 collective-permute-start.28
  341.6 3.5 collective-permute-start.29
  345.1 10.4 %collective-permute-done.26 = bf16[48,4096]{1,0:T(8,128)(2,1)S(1)} collective-permute-done((bf16[48,4096]{1,0:T(8,128)(2,1)S(1)}, bf16[48,4096]{1,0:T(8,128)(2,1)S(1)}, u32[]{:S(2)}, u32[]{:S(2)}) %collective-permute-start.26) | collective-permute-done | bytes 393248 | tf_op jit(solution)/shard_map/ppermute | solution.py:183
  355.5 1.8 collective-permute-done.27
  357.2 4.8 %collective-permute-done.28 = bf16[48,4096]{1,0:T(8,128)(2,1)S(1)} collective-permute-done((bf16[48,4096]{1,0:T(8,128)(2,1)S(1)}, bf16[48,4096]{1,0:T(8,128)(2,1)S(1)}, u32[]{:S(2)}, u32[]{:S(2)}) %collective-permute-start.28) | collective-permute-done | bytes 393248 | tf_op jit(solution)/shard_map/ppermute | solution.py:183
  362.0 9.8 %collective-permute-done.29 = bf16[48,4096]{1,0:T(8,128)(2,1)S(1)} collective-permute-done((bf16[48,4096]{1,0:T(8,128)(2,1)S(1)}, bf16[48,4096]{1,0:T(8,128)(2,1)S(1)}, u32[]{:S(2)}, u32[]{:S(2)}) %collective-permute-start.29) | collective-permute-done | bytes 393248 | tf_op jit(solution)/shard_map/ppermute | solution.py:183
  373.1 8.7 %all-to-all-start.1 = ((bf16[8,6,4096]{2,1,0:T(8,128)(2,1)}), bf16[8,6,4096]{2,1,0:T(8,128)(2,1)S(1)}, u32[]{:S(2)}, u32[]{:S(2)}) async-start(bf16[8,6,4096]{2,1,0:T(8,128)(2,1)} %reshape.223), calls=%async_computation.2 | async-start | bytes 1048576 | tf_op jit(solution)/shard_map/all_to_all | solution.py:185
  382.1 17.0 %all-to-all-done.1 = bf16[8,6,4096]{2,1,0:T(8,128)(2,1)S(1)} async-done(((bf16[8,6,4096]{2,1,0:T(8,128)(2,1)}), bf16[8,6,4096]{2,1,0:T(8,128)(2,1)S(1)}, u32[]{:S(2)}, u32[]{:S(2)}) %all-to-all-start.1) | async-done | bytes 393248 | tf_op jit(solution)/shard_map/all_to_all | solution.py:185
  (122 shorter events, 31.7 us)
Async XLA Ops:
  6.5 67.6 %copy-start = (bf16[1,4,128,2048]{3,2,1,0:T(8,128)(2,1)S(1)}, bf16[1,4,128,2048]{3,2,1,0:T(8,128)(2,1)}, u32[]{:S(2)}) copy-start(bf16[1,4,128,2048]{3,2,1,0:T(8,128)(2,1)} %param.13) | copy-start | bytes 6291460
  6.5 113.5 %reduce-scatter.2.cloned.1.call-start = ((), (), s32[]{:S(2)}) async-start(), calls=%async_computation.3 | async-start | bytes 1179648 | tf_op jit(solution)/shard_map/reduce_scatter | solution.py:128
  11.3 14.0 %collective-permute-start = (bf16[128,2048]{1,0:T(8,128)(2,1)}, bf16[128,2048]{1,0:T(8,128)(2,1)}, u32[]{:S(2)}, u32[]{:S(2)}) collective-permute-start(bf16[128,2048]{1,0:T(8,128)(2,1)} %constant_dynamic-slice_fusion.4), channel_id=1, source_target_pairs={{0,1},{1,0},{2,3},{3,2},{4,5},{5,4},{6,7},{7,6},{8,9},{9,8},{10,11... | collective-permute-start | bytes 1572872 | tf_op jit(solution)/shard_map/ppermute | solution.py:36
  18.1 16.3 %copy-start.2 = (bf16[2048,1,6,128]{0,3,2,1:T(8,128)(2,1)S(1)}, bf16[2048,1,6,128]{0,3,2,1:T(8,128)(2,1)}, u32[]{:S(2)}) copy-start(bf16[2048,1,6,128]{0,3,2,1:T(8,128)(2,1)} %copy.37) | copy-start | bytes 9437188
  28.5 5.9 %collective-permute-start.1 = (bf16[128,768]{1,0:T(8,128)(2,1)S(1)}, bf16[128,768]{1,0:T(8,128)(2,1)S(1)}, u32[]{:S(2)}, u32[]{:S(2)}) collective-permute-start(bf16[128,768]{1,0:T(8,128)(2,1)S(1)} %convolution_convert_fusion.4), channel_id=1, source_target_pairs={{0,1},{1,0},{2,3},{3,2},{4,5},{5,4},{6,7},{7,6},{8,9},{9,8},{10,11... | collective-permute-start | bytes 589832 | tf_op jit(solution)/shard_map/ppermute | solution.py:36
  37.1 15.8 %collective-permute-start.2 = (bf16[128,256]{1,0:T(8,128)(2,1)S(1)}, bf16[128,256]{1,0:T(8,128)(2,1)S(1)}, u32[]{:S(2)}, u32[]{:S(2)}) collective-permute-start(bf16[128,256]{1,0:T(8,128)(2,1)S(1)} %get-tuple-element.14), channel_id=1, source_target_pairs={{0,32},{32,64},{64,96},{96,128},{128,160},{160,192},{192,224},{1,3... | collective-permute-start | bytes 196616 | tf_op jit(solution)/shard_map/ppermute | solution.py:98
  40.6 13.7 %collective-permute-start.3 = (bf16[128,256]{1,0:T(8,128)(2,1)S(1)}, bf16[128,256]{1,0:T(8,128)(2,1)S(1)}, u32[]{:S(2)}, u32[]{:S(2)}) collective-permute-start(bf16[128,256]{1,0:T(8,128)(2,1)S(1)} %get-tuple-element.14), channel_id=1, source_target_pairs={{0,64},{32,96},{64,128},{96,160},{128,192},{160,224},{1,65},{33,97... | collective-permute-start | bytes 196616 | tf_op jit(solution)/shard_map/ppermute | solution.py:98
  46.3 8.7 %collective-permute-start.4 = (bf16[128,256]{1,0:T(8,128)(2,1)S(1)}, bf16[128,256]{1,0:T(8,128)(2,1)S(1)}, u32[]{:S(2)}, u32[]{:S(2)}) collective-permute-start(bf16[128,256]{1,0:T(8,128)(2,1)S(1)} %get-tuple-element.14), channel_id=1, source_target_pairs={{0,96},{32,128},{64,160},{96,192},{128,224},{1,97},{33,129},{65,16... | collective-permute-start | bytes 196616 | tf_op jit(solution)/shard_map/ppermute | solution.py:98
  50.3 4.7 %collective-permute-start.5 = (bf16[128,256]{1,0:T(8,128)(2,1)S(1)}, bf16[128,256]{1,0:T(8,128)(2,1)S(1)}, u32[]{:S(2)}, u32[]{:S(2)}) collective-permute-start(bf16[128,256]{1,0:T(8,128)(2,1)S(1)} %get-tuple-element.14), channel_id=1, source_target_pairs={{0,128},{32,160},{64,192},{96,224},{1,129},{33,161},{65,193},{97,2... | collective-permute-start | bytes 196616 | tf_op jit(solution)/shard_map/ppermute | solution.py:98
  51.6 3.4 collective-permute-start.6
  52.9 3.2 collective-permute-start.7
  54.3 1.9 collective-permute-start.8
  56.2 3.6 collective-permute-start.9
  61.8 3.2 copy-start.3
  61.8 3.2 copy-start.4
  61.8 3.2 copy-start.5
  68.0 7.9 %copy-start.7 = (bf16[4096]{0:T(1024)(128)(2,1)S(1)}, bf16[4096]{0:T(1024)(128)(2,1)}, u32[]{:S(2)}) copy-start(bf16[4096]{0:T(1024)(128)(2,1)} %param.14) | copy-start | bytes 24580
  68.0 7.9 %copy-start.8 = (s32[1,16,2]{1,2,0:T(2,128)S(1)}, s32[1,16,2]{1,2,0:T(2,128)}, u32[]{:S(2)}) copy-start(s32[1,16,2]{1,2,0:T(2,128)} %param.18) | copy-start | bytes 388
  68.0 7.9 %copy-start.9 = (s32[1,16,2]{1,2,0:T(2,128)S(1)}, s32[1,16,2]{1,2,0:T(2,128)}, u32[]{:S(2)}) copy-start(s32[1,16,2]{1,2,0:T(2,128)} %param.19) | copy-start | bytes 388
  68.2 6.0 %collective-permute-start.10 = (bf16[128,512]{1,0:T(8,128)(2,1)S(1)}, bf16[128,512]{1,0:T(8,128)(2,1)S(1)}, u32[]{:S(2)}, u32[]{:S(2)}) collective-permute-start(bf16[128,512]{1,0:T(8,128)(2,1)S(1)} %copy.48), channel_id=1, source_target_pairs={{0,1},{1,0},{2,3},{3,2},{4,5},{5,4},{6,7},{7,6},{8,9},{9,8},{10,11... | collective-permute-start | bytes 393224 | tf_op jit(solution)/shard_map/ppermute | solution.py:36
  120.9 4.5 %collective-permute-start.11 = (bf16[16,2048]{1,0:T(8,128)(2,1)S(1)}, bf16[16,2048]{1,0:T(8,128)(2,1)S(1)}, u32[]{:S(2)}, u32[]{:S(2)}) collective-permute-start(bf16[16,2048]{1,0:T(8,128)(2,1)S(1)} %get-tuple-element.35), channel_id=1, source_target_pairs={{0,1},{1,0},{2,3},{3,2},{4,5},{5,4},{6,7},{7,6},{8,9},{9,8},{10,11... | collective-permute-start | bytes 196616 | tf_op jit(solution)/shard_map/ppermute | solution.py:36
  126.9 17.8 %all-to-all-start = ((bf16[8,6,4096]{2,1,0:T(8,128)(2,1)}), bf16[8,6,4096]{2,1,0:T(8,128)(2,1)S(1)}, u32[]{:S(2)}, u32[]{:S(2)}) async-start(bf16[8,6,4096]{2,1,0:T(8,128)(2,1)} %reshape.220), calls=%async_computation.1 | async-start | bytes 1048576 | tf_op jit(solution)/shard_map/all_to_all | solution.py:161
  136.3 136.7 %collective-permute-start.20 = (bf16[2048,2,512]{2,0,1:T(8,128)(2,1)}, bf16[2048,2,512]{2,0,1:T(8,128)(2,1)}, u32[]{:S(2)}, u32[]{:S(2)}) collective-permute-start(bf16[2048,2,512]{2,0,1:T(8,128)(2,1)} %bitcast.159), channel_id=1, source_target_pairs={{0,1},{1,0},{2,3},{3,2},{4,5},{5,4},{6,7},{7,6},{8,9},{9,8},{10,11... | collective-permute-start | bytes 12582920 | tf_op jit(solution)/shard_map/ppermute | solution.py:36
  144.9 101.6 %collective-permute-start.12 = (bf16[48,4096]{1,0:T(8,128)(2,1)S(1)}, bf16[48,4096]{1,0:T(8,128)(2,1)S(1)}, u32[]{:S(2)}, u32[]{:S(2)}) collective-permute-start(bf16[48,4096]{1,0:T(8,128)(2,1)S(1)} %reshape.221), channel_id=1, source_target_pairs={{0,128},{32,160},{64,192},{96,224},{128,0},{160,32},{192,64},{224,... | collective-permute-start | bytes 1179656 | tf_op jit(solution)/shard_map/ppermute | solution.py:165
  148.0 99.3 %collective-permute-start.13 = (bf16[48,4096]{1,0:T(8,128)(2,1)S(1)}, bf16[48,4096]{1,0:T(8,128)(2,1)S(1)}, u32[]{:S(2)}, u32[]{:S(2)}) collective-permute-start(bf16[48,4096]{1,0:T(8,128)(2,1)S(1)} %reshape.221), channel_id=1, source_target_pairs={{0,32},{32,64},{64,96},{96,0},{128,160},{160,192},{192,224},{224,1... | collective-permute-start | bytes 1179656 | tf_op jit(solution)/shard_map/ppermute | solution.py:165
  149.3 100.5 %collective-permute-start.14 = (bf16[48,4096]{1,0:T(8,128)(2,1)S(1)}, bf16[48,4096]{1,0:T(8,128)(2,1)S(1)}, u32[]{:S(2)}, u32[]{:S(2)}) collective-permute-start(bf16[48,4096]{1,0:T(8,128)(2,1)S(1)} %reshape.221), channel_id=1, source_target_pairs={{0,96},{32,0},{64,32},{96,64},{128,224},{160,128},{192,160},{224,1... | collective-permute-start | bytes 1179656 | tf_op jit(solution)/shard_map/ppermute | solution.py:165
  150.0 103.3 %collective-permute-start.15 = (bf16[48,4096]{1,0:T(8,128)(2,1)S(1)}, bf16[48,4096]{1,0:T(8,128)(2,1)S(1)}, u32[]{:S(2)}, u32[]{:S(2)}) collective-permute-start(bf16[48,4096]{1,0:T(8,128)(2,1)S(1)} %reshape.221), channel_id=1, source_target_pairs={{0,160},{32,192},{64,224},{96,128},{128,32},{160,64},{192,96},{224... | collective-permute-start | bytes 1179656 | tf_op jit(solution)/shard_map/ppermute | solution.py:165
  246.5 11.7 %collective-permute-start.16 = (bf16[48,4096]{1,0:T(8,128)(2,1)S(1)}, bf16[48,4096]{1,0:T(8,128)(2,1)S(1)}, u32[]{:S(2)}, u32[]{:S(2)}) collective-permute-start(bf16[48,4096]{1,0:T(8,128)(2,1)S(1)} %reshape.221), channel_id=1, source_target_pairs={{0,224},{32,128},{64,160},{96,192},{128,96},{160,0},{192,32},{224,... | collective-permute-start | bytes 1179656 | tf_op jit(solution)/shard_map/ppermute | solution.py:165
  247.3 12.9 %collective-permute-start.17 = (bf16[48,4096]{1,0:T(8,128)(2,1)S(1)}, bf16[48,4096]{1,0:T(8,128)(2,1)S(1)}, u32[]{:S(2)}, u32[]{:S(2)}) collective-permute-start(bf16[48,4096]{1,0:T(8,128)(2,1)S(1)} %reshape.221), channel_id=1, source_target_pairs={{0,64},{32,96},{64,0},{96,32},{128,192},{160,224},{192,128},{224,1... | collective-permute-start | bytes 1179656 | tf_op jit(solution)/shard_map/ppermute | solution.py:165
  249.8 16.8 %collective-permute-start.18 = (bf16[48,4096]{1,0:T(8,128)(2,1)S(1)}, bf16[48,4096]{1,0:T(8,128)(2,1)S(1)}, u32[]{:S(2)}, u32[]{:S(2)}) collective-permute-start(bf16[48,4096]{1,0:T(8,128)(2,1)S(1)} %reshape.221), channel_id=1, source_target_pairs={{0,192},{32,224},{64,128},{96,160},{128,64},{160,96},{192,0},{224,... | collective-permute-start | bytes 1179656 | tf_op jit(solution)/shard_map/ppermute | solution.py:165
  266.6 5.7 %collective-permute-start.19 = (bf16[8,48,4096]{2,1,0:T(8,128)(2,1)S(1)}, bf16[8,48,4096]{2,1,0:T(8,128)(2,1)S(1)}, u32[]{:S(2)}, u32[]{:S(2)}) collective-permute-start(bf16[8,48,4096]{2,1,0:T(8,128)(2,1)S(1)} %bitcast_dynamic-update-slice_fusion), channel_id=1, source_target_pairs={{0,16},{16,0},{1,17},{17,1},{2,18},{18,2},{3,19},{19,3},{4,20},{20... | collective-permute-start | bytes 9437192 | tf_op jit(solution)/shard_map/ppermute | solution.py:40
  266.7 48.3 %collective-permute-start.21 = (bf16[512,2048]{1,0:T(8,128)(2,1)}, bf16[512,2048]{1,0:T(8,128)(2,1)}, u32[]{:S(2)}, u32[]{:S(2)}) collective-permute-start(bf16[512,2048]{1,0:T(8,128)(2,1)} %bitcast.53), channel_id=1, source_target_pairs={{0,1},{1,0},{2,3},{3,2},{4,5},{5,4},{6,7},{7,6},{8,9},{9,8},{10,11... | collective-permute-start | bytes 6291464 | tf_op jit(solution)/shard_map/ppermute | solution.py:36
  319.1 5.7 %collective-permute-start.22 = (bf16[8,48,4096]{2,1,0:T(8,128)(2,1)S(1)}, bf16[8,48,4096]{2,1,0:T(8,128)(2,1)S(1)}, u32[]{:S(2)}, u32[]{:S(2)}) collective-permute-start(bf16[8,48,4096]{2,1,0:T(8,128)(2,1)S(1)} %bitcast.168), channel_id=1, source_target_pairs={{0,16},{16,0},{1,17},{17,1},{2,18},{18,2},{3,19},{19,3},{4,20},{20... | collective-permute-start | bytes 9437192 | tf_op jit(solution)/shard_map/ppermute | solution.py:40
  326.3 55.5 %copy-start.6 = (bf16[4096,8]{0,1:T(8,128)(2,1)S(1)}, bf16[4096,8]{0,1:T(8,128)(2,1)}, u32[]{:S(2)}) copy-start(bf16[4096,8]{0,1:T(8,128)(2,1)} %param.15) | copy-start | bytes 196612
  326.3 12.7 %collective-permute-start.23 = (bf16[48,4096]{1,0:T(8,128)(2,1)S(1)}, bf16[48,4096]{1,0:T(8,128)(2,1)S(1)}, u32[]{:S(2)}, u32[]{:S(2)}) collective-permute-start(bf16[48,4096]{1,0:T(8,128)(2,1)S(1)} %get-tuple-element.17), channel_id=1, source_target_pairs={{128,0},{160,32},{192,64},{224,96},{0,128},{32,160},{64,192},{96,2... | collective-permute-start | bytes 1179656 | tf_op jit(solution)/shard_map/ppermute | solution.py:183
  327.2 14.4 %collective-permute-start.24 = (bf16[48,4096]{1,0:T(8,128)(2,1)S(1)}, bf16[48,4096]{1,0:T(8,128)(2,1)S(1)}, u32[]{:S(2)}, u32[]{:S(2)}) collective-permute-start(bf16[48,4096]{1,0:T(8,128)(2,1)S(1)} %get-tuple-element.23), channel_id=1, source_target_pairs={{32,0},{64,32},{96,64},{0,96},{160,128},{192,160},{224,192},{128,2... | collective-permute-start | bytes 1179656 | tf_op jit(solution)/shard_map/ppermute | solution.py:183
  327.2 17.9 %collective-permute-start.25 = (bf16[48,4096]{1,0:T(8,128)(2,1)S(1)}, bf16[48,4096]{1,0:T(8,128)(2,1)S(1)}, u32[]{:S(2)}, u32[]{:S(2)}) collective-permute-start(bf16[48,4096]{1,0:T(8,128)(2,1)S(1)} %get-tuple-element.22), channel_id=1, source_target_pairs={{96,0},{0,32},{32,64},{64,96},{224,128},{128,160},{160,192},{192,2... | collective-permute-start | bytes 1179656 | tf_op jit(solution)/shard_map/ppermute | solution.py:183
  329.2 26.2 %collective-permute-start.26 = (bf16[48,4096]{1,0:T(8,128)(2,1)S(1)}, bf16[48,4096]{1,0:T(8,128)(2,1)S(1)}, u32[]{:S(2)}, u32[]{:S(2)}) collective-permute-start(bf16[48,4096]{1,0:T(8,128)(2,1)S(1)} %get-tuple-element.21), channel_id=1, source_target_pairs={{160,0},{192,32},{224,64},{128,96},{32,128},{64,160},{96,192},{0,2... | collective-permute-start | bytes 1179656 | tf_op jit(solution)/shard_map/ppermute | solution.py:183
  333.0 24.2 %collective-permute-start.27 = (bf16[48,4096]{1,0:T(8,128)(2,1)S(1)}, bf16[48,4096]{1,0:T(8,128)(2,1)S(1)}, u32[]{:S(2)}, u32[]{:S(2)}) collective-permute-start(bf16[48,4096]{1,0:T(8,128)(2,1)S(1)} %get-tuple-element.20), channel_id=1, source_target_pairs={{224,0},{128,32},{160,64},{192,96},{96,128},{0,160},{32,192},{64,2... | collective-permute-start | bytes 1179656 | tf_op jit(solution)/shard_map/ppermute | solution.py:183
  339.1 22.9 %collective-permute-start.28 = (bf16[48,4096]{1,0:T(8,128)(2,1)S(1)}, bf16[48,4096]{1,0:T(8,128)(2,1)S(1)}, u32[]{:S(2)}, u32[]{:S(2)}) collective-permute-start(bf16[48,4096]{1,0:T(8,128)(2,1)S(1)} %get-tuple-element.19), channel_id=1, source_target_pairs={{64,0},{96,32},{0,64},{32,96},{192,128},{224,160},{128,192},{160,2... | collective-permute-start | bytes 1179656 | tf_op jit(solution)/shard_map/ppermute | solution.py:183
  341.6 30.2 %collective-permute-start.29 = (bf16[48,4096]{1,0:T(8,128)(2,1)S(1)}, bf16[48,4096]{1,0:T(8,128)(2,1)S(1)}, u32[]{:S(2)}, u32[]{:S(2)}) collective-permute-start(bf16[48,4096]{1,0:T(8,128)(2,1)S(1)} %get-tuple-element.18), channel_id=1, source_target_pairs={{192,0},{224,32},{128,64},{160,96},{64,128},{96,160},{0,192},{32,2... | collective-permute-start | bytes 1179656 | tf_op jit(solution)/shard_map/ppermute | solution.py:183
  371.8 28.5 %copy-start.1 = (bf16[1,4,128,2048]{3,2,1,0:T(8,128)(2,1)S(1)}, bf16[1,4,128,2048]{3,2,1,0:T(8,128)(2,1)}, u32[]{:S(2)}) copy-start(bf16[1,4,128,2048]{3,2,1,0:T(8,128)(2,1)} %param.13) | copy-start | bytes 6291460
  373.1 26.0 %all-to-all-start.1 = ((bf16[8,6,4096]{2,1,0:T(8,128)(2,1)}), bf16[8,6,4096]{2,1,0:T(8,128)(2,1)S(1)}, u32[]{:S(2)}, u32[]{:S(2)}) async-start(bf16[8,6,4096]{2,1,0:T(8,128)(2,1)} %reshape.223), calls=%async_computation.2 | async-start | bytes 1048576 | tf_op jit(solution)/shard_map/all_to_all | solution.py:185
Sparse Core Ops, SparseCore 0:
  76.0 43.9 reduce-scatter.1
